TPU v7x, 128 devices: a whole 4x4x4 slice. The times are simulated.
128 devices in a mesh: particle: 16 (over x, y_hi, core), classes: 4 (over z), orient: 2 (over y_lo).
Axes of the slice: x: 4, y: 4 (y_hi: 2, y_lo: 2; y = y_hi * 2 + y_lo), z: 4, core: 2. Of those that a mesh axis runs over, the one named last changes fastest.
Arguments:
- images: bfloat16 [12288, 16384], P('particle'), may hold values from -28 to 28, as said below
- ctf_table: float32 [8, 16384], replicated, may hold values from -1 to 1
- defocus: int32 [12288], P('particle'), may hold values from 0 to 7
- shifts: int32 [12288, 2], P('particle'), may hold values from -8 to 8
- noise_var: float32 [16384], replicated, may hold values from 0.5 to 4
- tau: float32 [16384], replicated, may hold values from 0.5 to 2
- bank: bfloat16 [8, 128, 16384], P('classes', ('particle', 'orient')), may hold values from -0.125 to 0.125
Outputs:
- recon: float32 [8, 128, 16384], P('classes', ('particle', 'orient'))
- loglik: float32 [12288], P('particle')
Inputs may be any that keep to these rules, and one draw needn't show every extreme that they name: `images`: rows may differ in scale.
All inputs are finite; a program needn't handle non-finite values.
Results may differ from a plain program's by a relative error of at most 0.02.
Values may be sent and summed in bfloat16 or wider, within the bound.
A program may use at most 256 MiB of HBM per device.

v0:
```python
import math

import jax
import jax.numpy as jnp
from jax import lax
from jax.sharding import PartitionSpec as P

BOX = 128


def shift_images(images, shifts):
    half = BOX // 2
    count = BOX * half
    index = jnp.arange(count, dtype=jnp.int32)
    freq_x = (index % half).astype(jnp.float32)
    row = index // half
    freq_y = jnp.where(row < half, row, row - BOX).astype(jnp.float32)
    angle = (
        2.0
        * math.pi
        / BOX
        * (
            shifts[:, 0:1].astype(jnp.float32) * freq_x[None, :]
            + shifts[:, 1:2].astype(jnp.float32) * freq_y[None, :]
        )
    )
    cosine = jnp.cos(angle)
    sine = jnp.sin(angle)
    real_part = images[:, :count].astype(jnp.float32)
    imag_part = images[:, count:].astype(jnp.float32)
    return jnp.concatenate(
        [real_part * cosine - imag_part * sine, real_part * sine + imag_part * cosine], axis=1
    )


def body(images, ctf_table, defocus, shifts, noise_var, tau, bank):
    shifted = shift_images(images, shifts)
    onehot = (defocus[:, None] == jnp.arange(ctf_table.shape[0], dtype=jnp.int32)[None, :]).astype(
        jnp.float32
    )
    ctf = jnp.dot(
        onehot, ctf_table, precision=lax.Precision.HIGHEST, preferred_element_type=jnp.float32
    )
    inverse = 1.0 / noise_var
    xs_rows = (shifted * ctf * inverse[None, :]).astype(jnp.bfloat16)
    cs_rows = (0.5 * ctf * ctf * inverse[None, :]).astype(jnp.bfloat16)
    xc_rows = (shifted * ctf).astype(jnp.bfloat16)
    offset = jnp.sum(0.5 * shifted * shifted * inverse[None, :], axis=1)
    piece = lax.all_gather(bank, "particle", axis=1, tiled=True)
    piece_f = piece.astype(jnp.float32)
    squared = (piece_f * piece_f).astype(jnp.bfloat16)
    part_scores = jnp.einsum(
        "ip,kjp->ikj", xs_rows, piece, preferred_element_type=jnp.float32
    ) - jnp.einsum("ip,kjp->ikj", cs_rows, squared, preferred_element_type=jnp.float32)
    local_top = jnp.max(part_scores, axis=(1, 2))
    top = lax.pmax(local_top, ("classes", "orient"))
    total = lax.psum(
        jnp.sum(jnp.exp(part_scores - top[:, None, None]), axis=(1, 2)), ("classes", "orient")
    )
    loglik = top + jnp.log(total) - offset
    weights = (jnp.exp(part_scores - top[:, None, None]) / total[:, None, None]).astype(
        jnp.bfloat16
    )
    data = lax.psum_scatter(
        jnp.einsum("ikj,ip->jkp", weights, xc_rows, preferred_element_type=jnp.float32).astype(
            jnp.bfloat16
        ),
        "particle",
        scatter_dimension=0,
        tiled=True,
    ).astype(jnp.float32)
    bins = jnp.einsum(
        "ib,ikj->jkb", onehot, weights.astype(jnp.float32), precision=lax.Precision.HIGHEST
    )
    power = ctf_table * ctf_table
    own_bins = lax.psum_scatter(bins, "particle", scatter_dimension=0, tiled=True)
    wgt = jnp.einsum("jkb,bp->jkp", own_bins, power, precision=lax.Precision.HIGHEST)
    recon = jnp.transpose(data / (wgt + tau[None, None, :]), (1, 0, 2))
    return (recon, loglik)


def solution(mesh):
    in_specs = (
        P("particle", None),
        P(),
        P("particle"),
        P("particle", None),
        P(),
        P(),
        P("classes", ("particle", "orient"), None),
    )
    out_specs = (P("classes", ("particle", "orient"), None), P("particle"))
    return jax.shard_map(body, mesh=mesh, in_specs=in_specs, out_specs=out_specs, check_vma=False)
```

profile of v0, /device:TPU:0, one launch (start us, length us, event | category | flops | bytes accessed | tf_op | source)
XLA Modules:
  0.0 442.7 jit_solution(16903688522373956946)
XLA Ops:
  7.2 0.0 all-gather.2.cloned.1.call-start
  7.2 1.9 copy.12
  9.1 0.0 all-gather.2.cloned.1.call-update
  9.2 0.0 all-reduce.4.cloned.1.call-start
  9.2 0.8 convert_reduce_fusion.1
  10.0 0.9 broadcast_divide_fusion
  10.9 25.9 %fusion.37 = f32[768,16384]{1,0:T(8,128)} fusion(f32[8,16384]{1,0:T(8,128)} %param.8, s32[768]{0:T(1024)} %param.9), kind=kOutput, calls=%fused_computation.54 | convolution fusion | flops 1207965696 | bytes 50859008 | tf_op jit(solution)/shard_map/dot_general | solution.py:41
  36.8 100.2 %fusion.5 = (f32[768,8192]{1,0:T(8,128)}, f32[768,8192]{1,0:T(8,128)}) fusion(f32[8192]{0:T(1024)S(1)} %get-tuple-element.9, f32[768]{0:T(1024)S(1)} %get-tuple-element.3, f32[8192]{0:T(1024)S(1)} %get-tuple-element.8, f32[768]{0:T(1024)S(1)} %get-tuple-element.2, bf16[768,16384]{1,0:T(8,128)(2,1)} %param.7), kind=kLoop, calls=%fused_computation.13 | loop fusion | flops 75497472 | bytes 75569152 | tf_op jit(solution)/shard_map/sub | solution.py:32
  137.0 0.0 all-gather.2.cloned.1.call-done
  137.0 41.2 %fusion.15 = f32[768,2,64]{0,2,1:T(8,128)S(1)} fusion(f32[16384]{0:T(1024)S(1)} %broadcast_divide_fusion, f32[768,16384]{1,0:T(8,128)} %fusion.37, f32[768,8192]{1,0:T(8,128)} %get-tuple-element.5, f32[768,8192]{1,0:T(8,128)} %get-tuple-element.4, bf16[2,64,16384]{2,0,1:T(2,128)(2,1)} %all-gather.2.cloned.1.call-done), kind=kOutput, calls=%fused_computation.23 | convolution fusion | flops 3271557120 | bytes 105316352 | tf_op jit(solution)/shard_map/ip,kjp->ikj/dot_general | solution.py:52
  178.2 25.3 %fusion.46 = (f32[768]{0:T(1024)S(1)}, f32[768,2,64]{0,2,1:T(8,128)S(1)}) fusion(f32[768,2,64]{0,2,1:T(8,128)S(1)} %fusion.15, bf16[2,64,16384]{2,0,1:T(2,128)(2,1)} %all-gather.2.cloned.1.call-done, f32[768,16384]{1,0:T(8,128)} %fusion.37, f32[16384]{0:T(1024)S(1)} %broadcast_divide_fusion), kind=kOutput, calls=%fused_computation.65 | convolution fusion | flops 3278044416 | bytes 55380992 | tf_op jit(solution)/shard_map/ip,kjp->ikj/dot_general | solution.py:54
  203.6 21.2 %pmax.7 = f32[768]{0:T(1024)S(1)} all-reduce(f32[768]{0:T(1024)S(1)} %get-tuple-element.6), channel_id=1, replica_groups=mesh['particle'=16,'classes'=4,'orient'=2] {'classes','orient'}, use_global_device_ids=true, to_apply=%region_1.2 | all-reduce | flops 768 | bytes 6144 | tf_op jit(solution)/shard_map/pmax | solution.py:56
  224.8 0.1 fusion.28
  224.9 16.0 %psum.7 = f32[768]{0:T(1024)S(1)} all-reduce(f32[768]{0:T(1024)S(1)} %fusion.28), channel_id=1, replica_groups=mesh['particle'=16,'classes'=4,'orient'=2] {'classes','orient'}, use_global_device_ids=true, to_apply=%region_3.4 | all-reduce | flops 768 | bytes 6144 | tf_op jit(solution)/shard_map/psum | solution.py:57
  240.9 0.1 divide_convert_fusion
  241.0 0.0 copy-start.3
  241.0 35.6 %fusion.9 = f32[16384,128]{0,1} fusion(bf16[768,128]{0,1:T(8,128)(2,1)S(1)} %bitcast.32, f32[768,16384]{1,0:T(8,128)} %fusion.37, f32[768,8192]{1,0:T(8,128)} %get-tuple-element.5, f32[768,8192]{1,0:T(8,128)} %get-tuple-element.4), kind=kOutput, calls=%fused_computation.17 | convolution fusion | flops 3258974208 | bytes 109248512
  276.6 5.8 %convert_bitcast_fusion = bf16[64,2,16384]{2,0,1:T(8,128)(2,1)} fusion(f32[16384,2,64]{0,2,1:T(8,128)} %bitcast.31), kind=kLoop, calls=%fused_computation.28 | loop fusion | flops 2097152 | bytes 12582912 | tf_op jit(solution)/shard_map/convert_element_type | solution.py:65
  282.4 0.0 all-reduce.4.cloned.1.call-update
  282.5 0.0 copy-done.3
  282.5 0.6 dynamic-slice
  283.7 0.0 copy-start.1
  283.7 0.0 copy-start
  283.7 0.0 copy-start.2
  283.8 19.1 %fusion.3 = f32[768]{0:T(1024)S(1)} fusion(f32[768,8192]{1,0:T(8,128)} %get-tuple-element.5, f32[768,8192]{1,0:T(8,128)} %get-tuple-element.4, f32[16384]{0:T(1024)S(1)} %broadcast_divide_fusion), kind=kLoop, calls=%fused_computation.5 | loop fusion | flops 62913792 | bytes 50400256 | tf_op jit(solution)/shard_map/reduce_sum | solution.py:48
  302.9 0.0 copy-done.1
  302.9 0.1 convolution_bitcast_fusion
  303.0 0.2 copy.15
  303.2 65.5 %all-reduce.1 = f32[64,2,8]{2,0,1:T(8,128)S(1)} all-reduce(f32[64,2,8]{2,0,1:T(8,128)S(1)} %copy.15), channel_id=3, replica_groups=mesh['particle'=16,'classes'=4,'orient'=2] {'particle'}, use_global_device_ids=true, to_apply=%region_5.6.clone | all-reduce | flops 1024 | bytes 8192
  368.7 0.6 add_subtract_fusion
  369.3 63.8 %all-reduce.4.cloned.1.call-done = bf16[64,2,16384]{2,0,1:T(8,128)(2,1)} async-done(((bf16[64,2,16384]{2,0,1:T(8,128)(2,1)}), bf16[64,2,16384]{2,0,1:T(8,128)(2,1)}) %all-reduce.4.cloned.1.call-update) | async-done | bytes 4194320
  433.1 0.0 copy-done
  433.1 0.0 copy-done.2
  433.1 2.7 fusion.18
  (1 shorter events, 0.0 us)
Async XLA Ops:
  7.2 129.9 %all-gather.2.cloned.1.call-start = ((), (), s32[]{:S(2)}) async-start(), calls=%async_computation | async-start | bytes 4456448 | tf_op jit(solution)/shard_map/all_gather | solution.py:49
  9.2 424.0 %all-reduce.4.cloned.1.call-start = ((), (), s32[]{:S(2)}) async-start(), calls=%async_computation.1 | async-start | bytes 8388608
  241.0 41.5 %copy-start.3 = (u32[128]{0:T(128)S(1)}, u32[128]{0:T(128)}, u32[]{:S(2)}) copy-start(u32[128]{0:T(128)} %constant.48) | copy-start | bytes 1540
  283.7 19.2 %copy-start.1 = (s32[768]{0:T(1024)S(1)}, s32[768]{0:T(1024)}, u32[]{:S(2)}) copy-start(s32[768]{0:T(1024)} %param.9) | copy-start | bytes 9220
  283.7 149.4 %copy-start = (f32[8,16384]{1,0:T(8,128)S(1)}, f32[8,16384]{1,0:T(8,128)}, u32[]{:S(2)}) copy-start(f32[8,16384]{1,0:T(8,128)} %param.8) | copy-start | bytes 1572868
  283.7 149.4 %copy-start.2 = (f32[16384]{0:T(1024)S(1)}, f32[16384]{0:T(1024)}, u32[]{:S(2)}) copy-start(f32[16384]{0:T(1024)} %param.12) | copy-start | bytes 196612
Sparse Core Ops, SparseCore 0:
  11.0 58.4 all-gather.1
  282.6 150.4 all-reduce.3
where the time goes:
time: 443 us
  matrix products  131 us (30%)
  other arithmetic  128 us (29%)
  blocking collectives  103 us (23%)
  waiting for transfers between devices  63.8 us (14%)
  between operations  14.8 us (3%)
    sub x1, other arithmetic, shift_images(): real_part * cosine - imag_part * sine  100 us
    unnamed x1, blocking collectives  65.5 us
    unnamed x3, waiting for transfers between devices  63.8 us
    dot_general x1, matrix products, body(): jnp.einsum('ip,kjp->ikj', xs_rows, piece, preferred_element_type=jnp.floa...  41.2 us
    unnamed x1, matrix products  35.6 us
    dot_general x1, matrix products, body(): jnp.dot(onehot, ctf_table, precision=lax.Precision.HIGHEST, preferred_ele...  25.9 us
    dot_general x1, matrix products, body(): jnp.einsum('ip,kjp->ikj', cs_rows, squared, preferred_element_type=jnp.fl...  25.3 us
    pmax x1, blocking collectives, body(): top = lax.pmax(local_top, ('classes', 'orient'))  21.2 us
  transfers between devices with their start and end apart: 2, of which 1 were waited for; matrix products, arithmetic and copies ran while one was open for 34% of the time, Pallas kernels for 0%

commit v1 on v0

v1 whole, which is shorter than its diff:
```python
import math

import jax
import jax.numpy as jnp
from jax import lax
from jax.experimental import pallas as pl
from jax.experimental.pallas import tpu as pltpu
from jax.sharding import PartitionSpec as P

MESH = pl.DeviceIdType.MESH
BOX = 128
F32 = jnp.float32
BF16 = jnp.bfloat16
NT = (((1,), (1,)), ((), ()))
CHUNKS = 8


def pick_rows(table, index):
    parts = [
        jnp.take_along_axis(table, index[s : s + 8], axis=0, mode="promise_in_bounds")
        for s in range(0, index.shape[0], 8)
    ]
    return parts[0] if len(parts) == 1 else jnp.concatenate(parts, axis=0)


def kernel(
    images, ctf, noise, tau, bank, cos0, sin0, rcos, rsin, bin_lanes, bin_row,
    recon, loglik,
    xc, gathered, cst, sst, off, acc, csq, scaled, squared, scores, wt, msg, msgs, binsend, binrecv, binsum,
    part, sib, ring, fin,
    img_sem, loc_sem, ysend, yrecv, rsend, rrecv, ssend, srecv,
    msend, mrecv, bsend, brecv, psend, precv, qsend, qrecv, fsend, frecv,
):
    rows, size = xc.shape
    half = size // 2
    width = half // CHUNKS
    tiles = width // 128

    me = lax.axis_index("particle")
    cls = lax.axis_index("classes")
    ori = lax.axis_index("orient")
    core = me % 2
    yh = (me // 2) % 2
    x = me // 4
    turn = 3 + 2 * core
    nxt = (((x + 1 + 2 * core) % 4) * 2 + yh) * 2 + core
    prv = (((x + 3 + 2 * core) % 4) * 2 + yh) * 2 + core
    sibling = me + 1 - 2 * core
    partner = me + 2 - 4 * yh
    own = core * 8 + x * 2 + yh
    share = cls * 2 + ori

    def cols(c, base=0):
        return pl.ds(pl.multiple_of(base + c * width, width), width)

    def img_copy(h, c):
        where = cols(c, h * half)
        return pltpu.make_async_copy(images.at[:, where], xc.at[:, where], img_sem.at[h, c])

    def start_images(c, _):
        img_copy(0, c).start()
        img_copy(1, c).start()
        return 0

    lax.fori_loop(0, CHUNKS, start_images, 0)

    def share_device(s):
        return {"classes": s // 2, "orient": s % 2}

    barrier = pltpu.get_barrier_semaphore()
    for k in range(1, 16):
        pl.semaphore_signal(barrier, inc=1, device_id={"particle": (me + k) % 16}, device_id_type=MESH)
    for k in range(1, 8):
        pl.semaphore_signal(barrier, inc=1, device_id=share_device((share + k) % 8), device_id_type=MESH)
    pl.semaphore_wait(barrier, 22)

    def remote(src, dst, send, recv, to):
        return pltpu.make_async_remote_copy(
            src_ref=src, dst_ref=dst, send_sem=send, recv_sem=recv, device_id=to, device_id_type=MESH
        )

    def y_copy(c):
        return remote(
            bank.at[:, cols(c)], gathered.at[own, :, cols(c)], ysend.at[c], yrecv.at[c], {"particle": partner}
        )

    def pair(t, c):
        return gathered.at[pl.ds(core * 8 + ((x + t * turn) % 4) * 2, 2), :, cols(c)]

    def ring_copy(t, c):
        return remote(pair(t, c), pair(t, c), rsend.at[t, c], rrecv.at[t, c], {"particle": nxt})

    def sib_copy(t, c):
        return remote(pair(t, c), pair(t, c), ssend.at[t, c], srecv.at[t, c], {"particle": sibling})

    def start_y(c, _):
        y_copy(c).start()
        return 0

    lax.fori_loop(0, CHUNKS, start_y, 0)
    mine = pltpu.make_async_copy(bank, gathered.at[own], loc_sem)
    mine.start()
    cst[...] = cos0[...]
    sst[...] = sin0[...]
    off[...] = jnp.zeros_like(off)
    acc[...] = jnp.zeros_like(acc)
    csq[...] = jnp.zeros_like(csq)
    mine.wait()

    def shift_chunk(c, with_offset):
        def group(g, _):
            where = pl.ds(pl.multiple_of(g * 16, 16), 16)
            cosine, sine = cst[where, :], sst[where, :]
            step_c, step_s = rcos[where, :], rsin[where, :]
            index = bin_lanes[where, :]
            total = off[where, :] if with_offset else None
            for j in range(tiles):
                at_re = pl.ds(pl.multiple_of(c * width + j * 128, 128), 128)
                at_im = pl.ds(pl.multiple_of(half + c * width + j * 128, 128), 128)
                re = xc[where, at_re].astype(F32)
                im = xc[where, at_im].astype(F32)
                out_re = re * cosine - im * sine
                out_im = re * sine + im * cosine
                if with_offset:
                    total = total + out_re * out_re * (0.5 / noise[:, at_re])
                    total = total + out_im * out_im * (0.5 / noise[:, at_im])
                xc[where, at_re] = (out_re * pick_rows(ctf[:, at_re], index)).astype(BF16)
                xc[where, at_im] = (out_im * pick_rows(ctf[:, at_im], index)).astype(BF16)
                cosine, sine = cosine * step_c - sine * step_s, sine * step_c + cosine * step_s
            cst[where, :] = cosine
            sst[where, :] = sine
            if with_offset:
                off[where, :] = total
            return 0

        lax.fori_loop(0, rows // 16, group, 0)

    def first(n, _):
        @pl.when(n < CHUNKS)
        def _():
            y_copy(n).wait_recv()
            ring_copy(0, n).start()
            sib_copy(0, n).start()

        for t in range(1, 4):
            c = n - t

            @pl.when((c >= 0) & (c < CHUNKS))
            def _():
                ring_copy(t - 1, c).wait_recv()
                if t < 3:
                    ring_copy(t, c).start()
                sib_copy(t, c).start()

        @pl.when(n < CHUNKS)
        def _():
            img_copy(0, n).wait()
            img_copy(1, n).wait()

            @pl.when(n == share)
            def _():
                shift_chunk(n, True)

            @pl.when(n != share)
            def _():
                shift_chunk(n, False)

        return 0

    lax.fori_loop(0, CHUNKS + 3, first, 0)

    def score(c, _):
        for t in range(4):
            sib_copy(t, c).wait_recv()
        for h in range(2):
            at = cols(c, h * half)
            inverse = 1.0 / noise[:, at]

            def prepare(m, _):
                b0 = gathered[2 * m, :, cols(c)].astype(F32)
                b1 = gathered[2 * m + 1, :, cols(c)].astype(F32)
                b = jnp.concatenate([b0[h * 8 : h * 8 + 8], b1[h * 8 : h * 8 + 8]], axis=0)
                value = b * inverse
                high = value.astype(BF16)
                to = pl.multiple_of(m * 16, 16)
                scaled[pl.ds(to, 16), h * width : (h + 1) * width] = high
                scaled[pl.ds(128 + to, 16), h * width : (h + 1) * width] = (value - high.astype(F32)).astype(BF16)
                squared[pl.ds(to, 16), h * width : (h + 1) * width] = (b * b).astype(BF16)
                return 0

            lax.fori_loop(0, 8, prepare, 0)
            table = ctf[:, at]
            cs = 0.5 * table * table * inverse
            cs = jnp.concatenate([cs, cs], axis=0).astype(BF16)
            csq[...] += lax.dot_general(
                cs, squared[:, h * width : (h + 1) * width], NT, preferred_element_type=F32
            )

        def block(r, _):
            where = pl.ds(pl.multiple_of(r * 256, 256), 256)
            acc[where, :] += lax.dot_general(
                xc[where, cols(c)], scaled[:, :width], NT, preferred_element_type=F32
            ) + lax.dot_general(xc[where, cols(c, half)], scaled[:, width:], NT, preferred_element_type=F32)
            return 0

        lax.fori_loop(0, rows // 256, block, 0)
        return 0

    lax.fori_loop(0, CHUNKS, score, 0)

    penalty = csq[0:8, :]
    for r in range(rows // 128):
        span = slice(r * 128, (r + 1) * 128)
        block_scores = acc[span, 0:128] + acc[span, 128:256] - pick_rows(penalty, bin_lanes[span, :])
        scores[:, span] = block_scores.T
        msg[2:3, span] = jnp.sum(off[span, :].T, axis=0, keepdims=True)
    local_top = jnp.max(scores[...], axis=0, keepdims=True)
    msg[0:1, :] = local_top
    msg[1:2, :] = jnp.sum(jnp.exp(scores[...] - local_top), axis=0, keepdims=True)
    msg[3:8, :] = jnp.zeros((5, rows), F32)

    def share_copy(k):
        return remote(msg, msgs.at[k], msend.at[k], mrecv.at[k], share_device((share + k) % 8))

    for k in range(1, 8):
        share_copy(k).start()
    msgs[0] = msg[...]
    for k in range(1, 8):
        share_copy(k).wait_recv()
    top = msgs[0, 0:1, :]
    for k in range(1, 8):
        top = jnp.maximum(top, msgs[k, 0:1, :])
    total = jnp.zeros_like(top)
    offset = jnp.zeros_like(top)
    for k in range(8):
        total = total + msgs[k, 1:2, :] * jnp.exp(msgs[k, 0:1, :] - top)
        offset = offset + msgs[k, 2:3, :]
    loglik[...] = top + jnp.log(total) - offset
    wt[...] = (jnp.exp(scores[...] - top) / total).astype(BF16)
    onehot = jnp.where(lax.broadcasted_iota(jnp.int32, (128, rows), 0) == bin_row[...], 1.0, 0.0).astype(BF16)
    bins = lax.dot_general(wt[...], onehot, NT, preferred_element_type=F32)
    for u in range(16):
        binsend[u] = bins[u * 8 : u * 8 + 8, :]

    def bin_copy(k):
        to = (me + k) % 16
        slot = (to % 2) * 8 + (to // 4) * 2 + (to // 2) % 2
        return remote(binsend.at[slot], binrecv.at[k], bsend.at[k], brecv.at[k], {"particle": to})

    for k in range(1, 16):
        bin_copy(k).start()

    def part_copy(c):
        return remote(
            part.at[pl.ds((1 - core) * 8, 8), :, cols(c)], sib.at[:, :, cols(c)],
            psend.at[c], precv.at[c], {"particle": sibling},
        )

    def target(t):
        return core * 8 + ((x + (1 + t) * turn) % 4) * 2

    def sum_copy(t, c):
        return remote(
            part.at[pl.ds(target(t), 2), :, cols(c)], ring.at[t, :, :, cols(c)],
            qsend.at[t, c], qrecv.at[t, c], {"particle": nxt},
        )

    def fin_copy(c):
        return remote(
            part.at[core * 8 + x * 2 + 1 - yh, :, cols(c)], fin.at[:, cols(c)],
            fsend.at[c], frecv.at[c], {"particle": partner},
        )

    sub = min(256, width)

    def second(n, _):
        @pl.when(n < CHUNKS)
        def _():
            def piece(s, _):
                at = pl.ds(pl.multiple_of(n * width + s * sub, sub), sub)
                at_im = pl.ds(pl.multiple_of(half + n * width + s * sub, sub), sub)
                re = jnp.dot(wt[...], xc[:, at], preferred_element_type=F32)
                im = jnp.dot(wt[...], xc[:, at_im], preferred_element_type=F32)
                for u in range(16):
                    span = slice(u * 8, u * 8 + 8)
                    part[u, :, at] = jnp.concatenate([re[span], im[span]], axis=0).astype(BF16)
                return 0

            lax.fori_loop(0, width // sub, piece, 0)
            part_copy(n).start()

        c = n - 1

        @pl.when((c >= 0) & (c < CHUNKS))
        def _():
            part_copy(c).wait_recv()

            def add(i, _):
                u = core * 8 + i
                part[u, :, cols(c)] = (
                    part[u, :, cols(c)].astype(F32) + sib[i, :, cols(c)].astype(F32)
                ).astype(BF16)
                return 0

            lax.fori_loop(0, 8, add, 0)
            sum_copy(0, c).start()

        for t in range(3):
            d = n - 2 - t

            @pl.when((d >= 0) & (d < CHUNKS))
            def _():
                sum_copy(t, d).wait_recv()
                for i in range(2):
                    u = target(t + 1) + i
                    part[u, :, cols(d)] = (
                        part[u, :, cols(d)].astype(F32) + ring[t, i, :, cols(d)].astype(F32)
                    ).astype(BF16)
                if t < 2:
                    sum_copy(t + 1, d).start()
                else:
                    fin_copy(d).start()

        @pl.when(n == 4)
        def _():
            whole = binsend[own]
            for k in range(1, 16):
                bin_copy(k).wait_recv()
                whole = whole + binrecv[k]
            binsum[...] = whole

        e = n - 5

        @pl.when((e >= 0) & (e < CHUNKS))
        def _():
            fin_copy(e).wait_recv()
            both = part[own, :, cols(e)].astype(F32) + fin[:, cols(e)].astype(F32)
            for h in range(2):
                at = cols(e, h * half)
                below = jnp.broadcast_to(tau[:, at], (8, width))
                for b in range(8):
                    value = ctf[b : b + 1, at]
                    below = below + binsum[:, b : b + 1] * (value * value)
                recon[:, at] = both[h * 8 : h * 8 + 8] / below

        return 0

    lax.fori_loop(0, CHUNKS + 5, second, 0)

    def finish(c, _):
        y_copy(c).wait_send()
        for t in range(3):
            ring_copy(t, c).wait_send()
            sum_copy(t, c).wait_send()
        for t in range(4):
            sib_copy(t, c).wait_send()
        part_copy(c).wait_send()
        fin_copy(c).wait_send()
        return 0

    lax.fori_loop(0, CHUNKS, finish, 0)
    for k in range(1, 8):
        share_copy(k).wait_send()
    for k in range(1, 16):
        bin_copy(k).wait_send()


def body(images, ctf_table, defocus, shifts, noise_var, tau, bank):
    rows, size = images.shape
    half = size // 2
    lane = jnp.arange(128, dtype=jnp.int32)
    turns = (shifts[:, 0:1] * (lane % 64)[None, :] + shifts[:, 1:2] * (lane // 64)[None, :]) % BOX
    angle = (2.0 * math.pi / BOX) * turns.astype(F32)
    step = jnp.broadcast_to((2.0 * math.pi / BOX) * ((2 * shifts[:, 1:2]) % BOX).astype(F32), (rows, 128))
    bin_lanes = jnp.broadcast_to(defocus[:, None], (rows, 128))
    shard = bank.reshape(8, 2, half).transpose(1, 0, 2).reshape(16, half)

    dma = pltpu.SemaphoreType.DMA
    vmem = pltpu.VMEM
    whole = pl.BlockSpec(memory_space=vmem)
    recon, loglik = pl.pallas_call(
        kernel,
        out_shape=(
            jax.ShapeDtypeStruct((8, size), F32),
            jax.ShapeDtypeStruct((1, rows), F32),
        ),
        in_specs=[pl.BlockSpec(memory_space=pl.ANY)] + [whole] * 10,
        out_specs=(whole, whole),
        scratch_shapes=[
            vmem((rows, size), BF16),
            vmem((16, 16, half), BF16),
            vmem((rows, 128), F32),
            vmem((rows, 128), F32),
            vmem((rows, 128), F32),
            vmem((rows, 256), F32),
            vmem((16, 128), F32),
            vmem((256, size // CHUNKS), BF16),
            vmem((128, size // CHUNKS), BF16),
            vmem((128, rows), F32),
            vmem((128, rows), BF16),
            vmem((8, rows), F32),
            vmem((8, 8, rows), F32),
            vmem((16, 8, 128), F32),
            vmem((16, 8, 128), F32),
            vmem((8, 128), F32),
            vmem((16, 16, half), BF16),
            vmem((8, 16, half), BF16),
            vmem((3, 2, 16, half), BF16),
            vmem((16, half), BF16),
            dma((2, CHUNKS)),
            dma,
            dma((CHUNKS,)),
            dma((CHUNKS,)),
            dma((3, CHUNKS)),
            dma((3, CHUNKS)),
            dma((4, CHUNKS)),
            dma((4, CHUNKS)),
            dma((8,)),
            dma((8,)),
            dma((16,)),
            dma((16,)),
            dma((CHUNKS,)),
            dma((CHUNKS,)),
            dma((3, CHUNKS)),
            dma((3, CHUNKS)),
            dma((CHUNKS,)),
            dma((CHUNKS,)),
        ],
        compiler_params=pltpu.CompilerParams(
            collective_id=0, has_side_effects=True, vmem_limit_bytes=60 * 1024 * 1024
        ),
        name="expectation",
    )(
        images, ctf_table, noise_var.reshape(1, size), tau.reshape(1, size), shard,
        jnp.cos(angle), jnp.sin(angle), jnp.cos(step), jnp.sin(step), bin_lanes, defocus.reshape(1, rows),
    )
    return recon.reshape(bank.shape), loglik.reshape(rows)


def solution(mesh):
    in_specs = (
        P("particle", None),
        P(),
        P("particle"),
        P("particle", None),
        P(),
        P(),
        P("classes", ("particle", "orient"), None),
    )
    out_specs = (P("classes", ("particle", "orient"), None), P("particle"))
    return jax.shard_map(body, mesh=mesh, in_specs=in_specs, out_specs=out_specs, check_vma=False)
```

time: 443 us -> 136 us (0.31)
  matrix products: 131 us -> 0 us
  other arithmetic: 128 us -> 4.98 us
  Pallas kernels: 0 us -> 121 us
  blocking collectives: 103 us -> 0 us
  waiting for transfers between devices: 63.8 us -> 0 us
  between operations: 14.8 us -> 0.66 us
  local copies, waits for them, and re-layouts: 2.71 us -> 9.62 us
    pallas_call x0 -> x1, Pallas kernels: none -> 121 us  [body(): pl.pallas_call(kernel, out_shape=(jax.ShapeDtypeStruct((8, size), F32), j...]
    sub x2 -> x0, other arithmetic: 101 us -> none  [the longest x1 100 us: shift_images(): real_part * cosine - imag_part * sine]
    dot_general x5 -> x0, matrix products: 95.3 us -> none  [the longest x1 41.2 us: body(): jnp.einsum('ip,kjp->ikj', xs_rows, piece, preferred_element_type=jnp.floa...]
    unnamed x1 -> x0, blocking collectives: 65.5 us -> none
    unnamed x3 -> x0, waiting for transfers between devices: 63.8 us -> none
    unnamed x1 -> x0, matrix products: 35.6 us -> none
    pmax x1 -> x0, blocking collectives: 21.2 us -> none  [body(): top = lax.pmax(local_top, ('classes', 'orient'))]
    reduce_sum x2 -> x0, other arithmetic: 19.2 us -> none  [the longest x1 19.1 us: body(): offset = jnp.sum(0.5 * shifted * shifted * inverse[None, :], axis=1)]
  transfers between devices with their start and end apart: 2 -> 0, of which waited for: 1 -> 0; matrix products, arithmetic and copies ran while one was open for 34% -> 0% of each run, Pallas kernels for 0% -> 0%
where the time goes in v1:
time: 136 us
  Pallas kernels  121 us (89%)
  local copies, waits for them, and re-layouts  9.62 us (7%)
  other arithmetic  4.98 us (4%)
    pallas_call x1, Pallas kernels, body(): pl.pallas_call(kernel, out_shape=(jax.ShapeDtypeStruct((8, size), F32), j...  121 us
    sin x1, other arithmetic, body(): jnp.sin(angle)  2.87 us

profile of v1, /device:TPU:0, one launch (start us, length us, event | category | flops | bytes accessed | tf_op | source)
XLA Modules:
  0.0 136.0 jit_solution(15179909850890658893)
XLA Ops:
  0.6 1.3 reshape.54.bin_row
  1.9 0.8 sine_reduce_fusion
  2.7 0.8 slice_reduce_fusion
  3.5 1.2 reshape.52
  4.8 0.9 copy.11
  5.6 0.9 broadcast_in_dim.7.rsin
  6.6 0.9 broadcast_in_dim.6.rcos
  7.5 1.6 %broadcast_in_dim.8.bin_lanes = s32[768,128]{1,0:T(8,128)} broadcast(s32[768]{0:T(1024)} %param.9), dimensions={0} | broadcast | bytes 396288 | tf_op jit(solution)/shard_map/broadcast_in_dim | solution.py:375
  9.1 2.9 %fusion.3 = (f32[768,128]{1,0:T(8,128)}, f32[768,128]{1,0:T(8,128)}) fusion(s32[128]{0:T(128)S(1)} %get-tuple-element.12, s32[768]{0:T(1024)S(1)} %get-tuple-element.7, s32[128]{0:T(128)S(1)} %get-tuple-element.13, s32[768]{0:T(1024)S(1)} %get-tuple-element.6), kind=kLoop, calls=%fused_computation.7 | loop fusion | flops 1572864 | bytes 793600 | tf_op jit(solution)/shard_map/sin | solution.py:435
  12.0 120.8 %expectation.1 = (f32[8,16384]{1,0:T(8,128)}, f32[1,768]{1,0:T(1,128)}) custom-call(bf16[768,16384]{1,0:T(8,128)(2,1)} %images.1, f32[8,16384]{1,0:T(8,128)} %ctf.1, f32[1,16384]{1,0:T(1,128)} %bitcast.8, f32[1,16384]{1,0:T(1,128)} %bitcast.9, bf16[16,8192]{1,0:T(8,128)(2,1)} %bitcast.7, f32[768,128]{1,0:T(8,128)} %get-tuple-element.11.cos0, ...), custom_call_target="tpu_custom_call" | custom-call | tf_op jit(solution)/shard_map/expectation/pallas_call | solution.py:381
  132.7 2.0 %reshape.55 = f32[2,4,16384]{2,1,0:T(4,128)} reshape(f32[8,16384]{1,0:T(8,128)} %get-tuple-element.4) | data formatting | bytes 1048576 | tf_op jit(solution)/shard_map/reshape | solution.py:437
  134.7 1.3 reduce.4
  (1 shorter events, 0.0 us)

commit v2 on v1

v2 whole, which is shorter than its diff:
```python
import jax
import jax.numpy as jnp
import numpy as np
from jax import lax
from jax.experimental import pallas as pl
from jax.experimental.pallas import tpu as pltpu
from jax.sharding import PartitionSpec as P

MESH = pl.DeviceIdType.MESH
BOX = 128
F32 = jnp.float32
BF16 = jnp.bfloat16
NT = (((1,), (1,)), ((), ()))
CHUNKS = 8
GROUP = 32


def pick_rows(table, index):
    parts = [
        jnp.take_along_axis(table, index[s : s + 8], axis=0, mode="promise_in_bounds")
        for s in range(0, index.shape[0], 8)
    ]
    return parts[0] if len(parts) == 1 else jnp.concatenate(parts, axis=0)


def kernel(
    images, ctf, noise, tau, bank, wave, moves, bin_row,
    recon, loglik,
    xc, gathered, cst, sst, rcos, rsin, bin_lanes, off, acc, csq, scaled, squared, scores, wt, msg, msgs, binsend, binrecv, binsum,
    part, sib, ring_a, ring_b, cross, fin,
    img_sem, ysend, yrecv, rsend, rrecv, ssend, srecv,
    msend, mrecv, bsend, brecv, psend, precv, qsend, arecv, brecv_ring, crecv, frecv,
):
    rows, size = xc.shape
    half = size // 2
    width = half // CHUNKS
    tiles = width // 128

    me = lax.axis_index("particle")
    cls = lax.axis_index("classes")
    ori = lax.axis_index("orient")
    core = me % 2
    yh = (me // 2) % 2
    x = me // 4
    turn = 3 + 2 * core
    nxt = (((x + 1 + 2 * core) % 4) * 2 + yh) * 2 + core
    prv = (((x + 3 + 2 * core) % 4) * 2 + yh) * 2 + core
    sibling = me + 1 - 2 * core
    partner = me + 2 - 4 * yh
    own = core * 8 + x * 2 + yh
    share = cls * 2 + ori

    def cols(c, base=0):
        return pl.ds(pl.multiple_of(base + c * width, width), width)

    def img_copy(h, c):
        where = cols(c, h * half)
        return pltpu.make_async_copy(images.at[:, where], xc.at[:, where], img_sem.at[h, c])

    def start_images(c, _):
        img_copy(0, c).start()
        img_copy(1, c).start()
        return 0

    lax.fori_loop(0, CHUNKS, start_images, 0)

    def share_device(s):
        return {"classes": s // 2, "orient": s % 2}

    def arrange(c, _):
        pieces = [bank[k, :, cols(c, h * half)].astype(F32) for h in range(2) for k in range(2)]
        gathered[own, :, cols(c)] = jnp.concatenate(pieces, axis=0).astype(BF16)
        return 0

    lax.fori_loop(0, CHUNKS, arrange, 0)

    barrier = pltpu.get_barrier_semaphore()
    for k in range(1, 16):
        pl.semaphore_signal(barrier, inc=1, device_id={"particle": (me + k) % 16}, device_id_type=MESH)
    for k in range(1, 8):
        pl.semaphore_signal(barrier, inc=1, device_id=share_device((share + k) % 8), device_id_type=MESH)
    pl.semaphore_wait(barrier, 22)

    def remote(src, dst, send, recv, to):
        return pltpu.make_async_remote_copy(
            src_ref=src, dst_ref=dst, send_sem=send, recv_sem=recv, device_id=to, device_id_type=MESH
        )

    def y_copy(c, q=None):
        q = cols(c) if q is None else q
        return remote(
            gathered.at[own, :, q], gathered.at[own, :, q], ysend, yrecv.at[c], {"particle": partner}
        )

    def pair(t, q):
        return gathered.at[pl.ds(core * 8 + ((x + t * turn) % 4) * 2, 2), :, q]

    def ring_copy(t, c, q=None):
        q = cols(c) if q is None else q
        return remote(pair(t, q), pair(t, q), rsend.at[t], rrecv.at[t, c], {"particle": nxt})

    def sib_copy(t, c, q=None):
        q = cols(c) if q is None else q
        return remote(pair(t, q), pair(t, q), ssend.at[t], srecv.at[t, c], {"particle": sibling})

    def start_y(c, _):
        y_copy(c).start()
        return 0

    lax.fori_loop(0, CHUNKS, start_y, 0)

    lane = lax.broadcasted_iota(jnp.int32, (128, 128), 1)

    waves = jnp.broadcast_to(wave[...], (8, BOX))

    def look(turns):
        turns = turns & (BOX - 1)
        return jnp.concatenate(
            [
                jnp.take_along_axis(waves, turns[s : s + 8], axis=1, mode="promise_in_bounds")
                for s in range(0, 128, 8)
            ],
            axis=0,
        )

    def phases(r, _):
        span = pl.ds(pl.multiple_of(r * 128, 128), 128)
        shift_x, shift_y, bins_of = [
            jnp.broadcast_to(row.astype(F32), (128, 128)).T.astype(jnp.int32)
            for row in (moves[0:1, span], moves[1:2, span], bin_row[:, span])
        ]
        turns = shift_x * (lane % 64) + shift_y * (lane // 64)
        cst[span, :] = look(turns)
        sst[span, :] = look(turns - BOX // 4)
        rcos[span, :] = look(2 * shift_y)
        rsin[span, :] = look(2 * shift_y - BOX // 4)
        bin_lanes[span, :] = bins_of
        return 0

    lax.fori_loop(0, rows // 128, phases, 0)
    off[...] = jnp.zeros_like(off)
    acc[...] = jnp.zeros_like(acc)
    csq[...] = jnp.zeros_like(csq)

    def shift_chunk(c, part_of, with_offset):
        lows = [pl.multiple_of(c * width + j * 128, 128) for j in range(tiles)]

        def group(g, _):
            where = pl.ds(pl.multiple_of(g * GROUP, GROUP), GROUP)
            cosine, sine = cst[where, :], sst[where, :]
            step_c, step_s = rcos[where, :], rsin[where, :]
            index = bin_lanes[where, :]
            total = off[where, :] if with_offset else None
            for low in lows:
                at_re = pl.ds(low, 128)
                at_im = pl.ds(pl.multiple_of(half + low, 128), 128)
                re = xc[where, at_re].astype(F32)
                im = xc[where, at_im].astype(F32)
                out_re = re * cosine - im * sine
                out_im = re * sine + im * cosine
                if with_offset:
                    total = total + out_re * out_re * (0.5 / noise[:, at_re])
                    total = total + out_im * out_im * (0.5 / noise[:, at_im])
                xc[where, at_re] = (out_re * pick_rows(ctf[:, at_re], index)).astype(BF16)
                xc[where, at_im] = (out_im * pick_rows(ctf[:, at_im], index)).astype(BF16)
                cosine, sine = cosine * step_c - sine * step_s, sine * step_c + cosine * step_s
            cst[where, :] = cosine
            sst[where, :] = sine
            if with_offset:
                off[where, :] = total
            return 0

        per = rows // GROUP // 2
        lax.fori_loop(part_of * per, part_of * per + per, group, 0)

    def score(c):
        for t in range(4):
            sib_copy(t, c).wait_recv()
        for h in range(2):
            at = cols(c, h * half)
            inverse = 1.0 / noise[:, at]

            def prepare(m, _):
                b0 = gathered[2 * m, :, cols(c)].astype(F32)
                b1 = gathered[2 * m + 1, :, cols(c)].astype(F32)
                b = jnp.concatenate([b0[h * 8 : h * 8 + 8], b1[h * 8 : h * 8 + 8]], axis=0)
                value = b * inverse
                high = value.astype(BF16)
                to = pl.multiple_of(m * 16, 16)
                scaled[pl.ds(to, 16), h * width : (h + 1) * width] = high
                scaled[pl.ds(128 + to, 16), h * width : (h + 1) * width] = (value - high.astype(F32)).astype(BF16)
                squared[pl.ds(to, 16), h * width : (h + 1) * width] = (b * b).astype(BF16)
                return 0

            lax.fori_loop(0, 8, prepare, 0)
            table = ctf[:, at]
            cs = 0.5 * table * table * inverse
            cs = jnp.concatenate([cs, cs], axis=0).astype(BF16)
            csq[...] += lax.dot_general(
                cs, squared[:, h * width : (h + 1) * width], NT, preferred_element_type=F32
            )

        def block(r, _):
            where = pl.ds(pl.multiple_of(r * 384, 384), 384)
            acc[where, :] += lax.dot_general(
                xc[where, cols(c)], scaled[:, :width], NT, preferred_element_type=F32
            ) + lax.dot_general(xc[where, cols(c, half)], scaled[:, width:], NT, preferred_element_type=F32)
            return 0

        lax.fori_loop(0, rows // 384, block, 0)

    def first(n, _):
        @pl.when(n < CHUNKS)
        def _():
            y_copy(n).wait_recv()
            ring_copy(0, n).start()
            sib_copy(0, n).start()

        for t in range(1, 4):
            c = n - 2 * t

            @pl.when((c >= 0) & (c < CHUNKS))
            def _():
                ring_copy(t - 1, c).wait_recv()
                if t < 3:
                    ring_copy(t, c).start()
                sib_copy(t, c).start()

        c = n // 2
        part_of = n % 2

        @pl.when(part_of == 0)
        def _():
            img_copy(0, c).wait()
            img_copy(1, c).wait()

        @pl.when(c == share)
        def _():
            shift_chunk(c, part_of, True)

        @pl.when(c != share)
        def _():
            shift_chunk(c, part_of, False)

        @pl.when(n >= CHUNKS)
        def _():
            score(n - CHUNKS)

        return 0

    lax.fori_loop(0, 2 * CHUNKS, first, 0)


    penalty = csq[0:8, :]
    for r in range(rows // 128):
        span = slice(r * 128, (r + 1) * 128)
        block_scores = acc[span, 0:128] + acc[span, 128:256] - pick_rows(penalty, bin_lanes[span, :])
        scores[:, span] = block_scores.T
        msg[2:3, span] = jnp.sum(off[span, :].T, axis=0, keepdims=True)
    local_top = jnp.max(scores[...], axis=0, keepdims=True)
    msg[0:1, :] = local_top
    msg[1:2, :] = jnp.sum(jnp.exp(scores[...] - local_top), axis=0, keepdims=True)
    msg[3:8, :] = jnp.zeros((5, rows), F32)

    def share_copy(k):
        return remote(msg, msgs.at[k], msend.at[k], mrecv.at[k], share_device((share + k) % 8))

    for k in range(1, 8):
        share_copy(k).start()
    msgs[0] = msg[...]
    for k in range(1, 8):
        share_copy(k).wait_recv()
    top = msgs[0, 0:1, :]
    for k in range(1, 8):
        top = jnp.maximum(top, msgs[k, 0:1, :])
    total = jnp.zeros_like(top)
    offset = jnp.zeros_like(top)
    for k in range(8):
        total = total + msgs[k, 1:2, :] * jnp.exp(msgs[k, 0:1, :] - top)
        offset = offset + msgs[k, 2:3, :]
    loglik[...] = top + jnp.log(total) - offset
    wt[...] = (jnp.exp(scores[...] - top) / total).astype(BF16)
    onehot = jnp.where(lax.broadcasted_iota(jnp.int32, (128, rows), 0) == bin_row[...], 1.0, 0.0).astype(BF16)
    bins = lax.dot_general(wt[...], onehot, NT, preferred_element_type=F32)
    for u in range(16):
        binsend[u] = bins[u * 8 : u * 8 + 8, :]

    def bin_copy(k):
        to = (me + k) % 16
        slot = (to % 2) * 8 + (to // 4) * 2 + (to // 2) % 2
        return remote(binsend.at[slot], binrecv.at[k], bsend.at[k], brecv.at[k], {"particle": to})

    for k in range(1, 16):
        bin_copy(k).start()

    steps = CHUNKS
    middle = half // 2
    span_of = middle // steps
    sub = min(256, span_of)

    def at_step(route, d):
        return pl.ds(pl.multiple_of(route * middle + d * span_of, span_of), span_of)

    def local(d):
        return pl.ds(pl.multiple_of(d * span_of, span_of), span_of)

    def everything(route):
        return pl.ds(route * middle, middle)

    def target(t):
        return (x + (1 + t) * turn) % 4

    def part_copy(route, d, q=None):
        q = at_step(route, d) if q is None else q
        return remote(
            part.at[1 - core, :, :, :, q], sib.at[:, :, :, q],
            psend.at[route], precv.at[route, d], {"particle": sibling},
        )

    def ring_a_copy(t, d, q=None):
        p = local(d) if q is None else q
        q = at_step(0, d) if q is None else q
        return remote(
            part.at[core, target(t), :, :, q], ring_a.at[t, :, :, p],
            qsend.at[t], arecv.at[t, d], {"particle": nxt},
        )

    def fin_copy(d, q=None):
        p = local(d) if q is None else q
        q = at_step(0, d) if q is None else q
        return remote(
            part.at[core, x, 1 - yh, :, q], fin.at[:, p], qsend.at[3], frecv.at[d], {"particle": partner}
        )

    def cross_copy(d, whole=False):
        p = everything(0) if whole else local(d)
        q = everything(1) if whole else at_step(1, d)
        return remote(
            part.at[core, :, 1 - yh, :, q], cross.at[:, :, p], qsend.at[4], crecv.at[d], {"particle": partner}
        )

    def ring_b_copy(t, d, whole=False):
        p = everything(0) if whole else local(d)
        q = everything(1) if whole else at_step(1, d)
        return remote(
            part.at[core, target(t), yh, :, q], ring_b.at[t, :, p],
            qsend.at[5 + t], brecv_ring.at[t, d], {"particle": nxt},
        )

    def gain(i, j, q, other):
        part[core, i, j, :, q] = (part[core, i, j, :, q].astype(F32) + other.astype(F32)).astype(BF16)

    def result(route, d, other):
        q = at_step(route, d)
        both = part[core, x, yh, :, q].astype(F32) + other.astype(F32)
        for h in range(2):
            at = pl.ds(pl.multiple_of(h * half + route * middle + d * span_of, span_of), span_of)
            below = jnp.broadcast_to(tau[:, at], (8, span_of))
            for b in range(8):
                value = ctf[b : b + 1, at]
                below = below + binsum[:, b : b + 1] * (value * value)
            value = both[h * 8 : h * 8 + 8] / below
            recon[0, :, at] = value[0:4]
            recon[1, :, at] = value[4:8]

    def stage(n, lag):
        d = n - lag
        return d, pl.when((d >= 0) & (d < steps))

    def second(n, _):
        @pl.when(n < steps)
        def _():
            per = span_of // sub

            def piece(s, _):
                low = (s // per) * middle + n * span_of + (s % per) * sub
                at = pl.ds(pl.multiple_of(low, sub), sub)
                at_im = pl.ds(pl.multiple_of(half + low, sub), sub)
                re = jnp.dot(wt[...], xc[:, at], preferred_element_type=F32)
                im = jnp.dot(wt[...], xc[:, at_im], preferred_element_type=F32)
                for u in range(16):
                    span = slice(u * 8, u * 8 + 8)
                    part[u // 8, (u // 2) % 4, u % 2, :, at] = jnp.concatenate(
                        [re[span], im[span]], axis=0
                    ).astype(BF16)
                return 0

            lax.fori_loop(0, 2 * per, piece, 0)
            part_copy(0, n).start()
            part_copy(1, n).start()

        d1, on1 = stage(n, 1)

        @on1
        def _():
            for route in range(2):
                part_copy(route, d1).wait_recv()
                q = at_step(route, d1)

                def add(i, _):
                    for j in range(2):
                        gain(i, j, q, sib[i, j, :, q])
                    return 0

                lax.fori_loop(0, 4, add, 0)
                if route == 0:
                    ring_a_copy(0, d1).start()
                else:
                    cross_copy(d1).start()

        d2, on2 = stage(n, 3)

        @on2
        def _():
            ring_a_copy(0, d2).wait_recv()
            for j in range(2):
                gain(target(1), j, at_step(0, d2), ring_a[0, j, :, local(d2)])
            ring_a_copy(1, d2).start()
            cross_copy(d2).wait_recv()
            for i in range(4):
                gain(i, yh, at_step(1, d2), cross[i, :, local(d2)])
            ring_b_copy(0, d2).start()

        d3, on3 = stage(n, 5)

        @on3
        def _():
            ring_a_copy(1, d3).wait_recv()
            for j in range(2):
                gain(target(2), j, at_step(0, d3), ring_a[1, j, :, local(d3)])
            ring_a_copy(2, d3).start()
            ring_b_copy(0, d3).wait_recv()
            gain(target(1), yh, at_step(1, d3), ring_b[0, :, local(d3)])
            ring_b_copy(1, d3).start()

        d4, on4 = stage(n, 7)

        @on4
        def _():
            ring_a_copy(2, d4).wait_recv()
            for j in range(2):
                gain(x, j, at_step(0, d4), ring_a[2, j, :, local(d4)])
            fin_copy(d4).start()
            ring_b_copy(1, d4).wait_recv()
            gain(target(2), yh, at_step(1, d4), ring_b[1, :, local(d4)])
            ring_b_copy(2, d4).start()

        @pl.when(n == 5)
        def _():
            whole = binsend[own]
            for k in range(1, 16):
                bin_copy(k).wait_recv()
                whole = whole + binrecv[k]
            binsum[...] = whole

        d5, on5 = stage(n, 9)

        @on5
        def _():
            fin_copy(d5).wait_recv()
            result(0, d5, fin[:, local(d5)])
            ring_b_copy(2, d5).wait_recv()
            result(1, d5, ring_b[2, :, local(d5)])

        return 0

    lax.fori_loop(0, steps + 9, second, 0)

    full = pl.ds(0, half)
    y_copy(0, full).wait_send()
    for t in range(3):
        ring_copy(t, 0, full).wait_send()
        ring_a_copy(t, 0, everything(0)).wait_send()
        ring_b_copy(t, 0, True).wait_send()
    for t in range(4):
        sib_copy(t, 0, full).wait_send()
    for route in range(2):
        part_copy(route, 0, everything(route)).wait_send()
    fin_copy(0, everything(0)).wait_send()
    cross_copy(0, True).wait_send()
    for k in range(1, 8):
        share_copy(k).wait_send()
    for k in range(1, 16):
        bin_copy(k).wait_send()


def body(images, ctf_table, defocus, shifts, noise_var, tau, bank):
    rows, size = images.shape
    half = size // 2
    wave = np.cos(2.0 * np.pi / BOX * np.arange(BOX)).astype(np.float32)
    wave = jnp.asarray(wave[None, :])

    dma = pltpu.SemaphoreType.DMA
    vmem = pltpu.VMEM
    whole = pl.BlockSpec(memory_space=vmem)
    recon, loglik = pl.pallas_call(
        kernel,
        out_shape=(
            jax.ShapeDtypeStruct(bank.shape, F32),
            jax.ShapeDtypeStruct((1, rows), F32),
        ),
        in_specs=[pl.BlockSpec(memory_space=pl.ANY)] + [whole] * 7,
        out_specs=(whole, whole),
        scratch_shapes=[
            vmem((rows, size), BF16),
            vmem((16, 16, half), BF16),
            vmem((rows, 128), F32),
            vmem((rows, 128), F32),
            vmem((rows, 128), F32),
            vmem((rows, 128), F32),
            vmem((rows, 128), jnp.int32),
            vmem((rows, 128), F32),
            vmem((rows, 256), F32),
            vmem((16, 128), F32),
            vmem((256, size // CHUNKS), BF16),
            vmem((128, size // CHUNKS), BF16),
            vmem((128, rows), F32),
            vmem((128, rows), BF16),
            vmem((8, rows), F32),
            vmem((8, 8, rows), F32),
            vmem((16, 8, 128), F32),
            vmem((16, 8, 128), F32),
            vmem((8, 128), F32),
            vmem((2, 4, 2, 16, half), BF16),
            vmem((4, 2, 16, half), BF16),
            vmem((3, 2, 16, half // 2), BF16),
            vmem((3, 16, half // 2), BF16),
            vmem((4, 16, half // 2), BF16),
            vmem((16, half // 2), BF16),
            dma((2, CHUNKS)),
            dma,
            dma((CHUNKS,)),
            dma((3,)),
            dma((3, CHUNKS)),
            dma((4,)),
            dma((4, CHUNKS)),
            dma((8,)),
            dma((8,)),
            dma((16,)),
            dma((16,)),
            dma((2,)),
            dma((2, CHUNKS)),
            dma((8,)),
            dma((3, CHUNKS)),
            dma((3, CHUNKS)),
            dma((CHUNKS,)),
            dma((CHUNKS,)),
        ],
        compiler_params=pltpu.CompilerParams(
            collective_id=0, has_side_effects=True, vmem_limit_bytes=60 * 1024 * 1024
        ),
        name="expectation",
    )(
        images, ctf_table, noise_var.reshape(1, size), tau.reshape(1, size), bank, wave,
        shifts.T, defocus[None, :],
    )
    return recon, loglik.reshape(rows)


def solution(mesh):
    in_specs = (
        P("particle", None),
        P(),
        P("particle"),
        P("particle", None),
        P(),
        P(),
        P("classes", ("particle", "orient"), None),
    )
    out_specs = (P("classes", ("particle", "orient"), None), P("particle"))
    return jax.shard_map(body, mesh=mesh, in_specs=in_specs, out_specs=out_specs, check_vma=False)
```

time: 136 us -> 99.1 us (0.73)
  Pallas kernels: 121 us -> 93.8 us
  local copies, waits for them, and re-layouts: 9.62 us -> 3.14 us
  other arithmetic: 4.98 us -> 1.29 us
    pallas_call x1, Pallas kernels: 121 us -> 93.8 us  [body(): pl.pallas_call(kernel, out_shape=(jax.ShapeDtypeStruct(bank.shape, F32),...]
    reshape x4 -> x0, local copies, waits for them, and re-layouts: 5.37 us -> none  [the longest x2 2.11 us: body(): shard = bank.reshape(8, 2, half).transpose(1, 0, 2).reshape(16, half)]
    sin x2 -> x0, other arithmetic: 3.69 us -> none  [the longest x1 2.87 us: body(): jnp.sin(angle)]
    broadcast_in_dim x3 -> x1, local copies, waits for them, and re-layouts: 3.46 us -> 1.27 us  [body(): defocus[None, :]]
    unnamed x0 -> x1, local copies, waits for them, and re-layouts: none -> 1.87 us
where the time goes in v2:
time: 99.1 us; the launch traced here: 98.9 us
  Pallas kernels  93.8 us (95%)
  local copies, waits for them, and re-layouts  3.14 us (3%)
  other arithmetic  1.29 us (1%)
    pallas_call x1, Pallas kernels, body(): pl.pallas_call(kernel, out_shape=(jax.ShapeDtypeStruct(bank.shape, F32),...  93.8 us

profile of v2, /device:TPU:0, one launch (start us, length us, event | category | flops | bytes accessed | tf_op | source)
XLA Modules:
  0.0 98.9 jit_solution(15002479182216337634)
XLA Ops:
  0.6 1.3 %broadcast_in_dim.3.bin_row = s32[1,768]{1,0:T(1,128)} reshape(s32[768]{0:T(1024)} %param.10) | data formatting | bytes 6144 | tf_op jit(solution)/shard_map/broadcast_in_dim | solution.py:555
  1.9 93.8 %expectation.1 = (f32[2,4,16384]{2,1,0:T(4,128)}, f32[1,768]{1,0:T(1,128)}) custom-call(bf16[768,16384]{1,0:T(8,128)(2,1)} %images.1, f32[8,16384]{1,0:T(8,128)} %ctf.1, f32[1,16384]{1,0:T(1,128)} %bitcast.3, f32[1,16384]{1,0:T(1,128)} %bitcast.4, bf16[2,4,16384]{2,1,0:T(4,128)(2,1)} %bank.1, f32[1,128]{1,0:T(1,128)} %constant.2.clone.wave, ...), custom_call_target="tpu_custom_call" | custom-call | tf_op jit(solution)/shard_map/expectation/pallas_call | solution.py:496
  95.7 1.3 %reduce = f32[768]{0:T(1024)} reduce(f32[1,768]{1,0:T(1,128)} %get-tuple-element.5, f32[]{:T(128)} %constant.4), dimensions={0}, to_apply=%get-tuple-element.5.reduce_sub_computation | reduce | bytes 6148 | tf_op jit(solution)/shard_map/expectation/pallas_call | solution.py:496
  97.0 1.9 %copy.11 = f32[2,4,16384]{2,1,0:T(4,128)} copy(f32[2,4,16384]{2,1,0:T(4,128)} %get-tuple-element.8) | data formatting | bytes 1048576

commit v3 on v2

--- a/solution.py
+++ b/solution.py
@@ -13,6 +13,8 @@
 NT = (((1,), (1,)), ((), ()))
 CHUNKS = 8
 GROUP = 32
+LAG = 3
+SCORE_ROWS = 768
 
 
 def pick_rows(table, index):
@@ -62,7 +64,7 @@
         img_copy(1, c).start()
         return 0
 
-    lax.fori_loop(0, CHUNKS, start_images, 0)
+    lax.fori_loop(0, 2, start_images, 0)
 
     def share_device(s):
         return {"classes": s // 2, "orient": s % 2}
@@ -97,7 +99,8 @@
 
     def ring_copy(t, c, q=None):
         q = cols(c) if q is None else q
-        return remote(pair(t, q), pair(t, q), rsend.at[t], rrecv.at[t, c], {"particle": nxt})
+        block = pair(1 if t == 2 else 0, q)
+        return remote(block, block, rsend.at[t], rrecv.at[t, c], {"particle": prv if t == 1 else nxt})
 
     def sib_copy(t, c, q=None):
         q = cols(c) if q is None else q
@@ -127,7 +130,7 @@
         span = pl.ds(pl.multiple_of(r * 128, 128), 128)
         shift_x, shift_y, bins_of = [
             jnp.broadcast_to(row.astype(F32), (128, 128)).T.astype(jnp.int32)
-            for row in (moves[0:1, span], moves[1:2, span], bin_row[:, span])
+            for row in (moves[0:1, span], moves[1:2, span], bin_row[span].reshape(1, 128))
         ]
         turns = shift_x * (lane % 64) + shift_y * (lane // 64)
         cst[span, :] = look(turns)
@@ -201,55 +204,69 @@
             )
 
         def block(r, _):
-            where = pl.ds(pl.multiple_of(r * 384, 384), 384)
+            where = pl.ds(pl.multiple_of(r * SCORE_ROWS, SCORE_ROWS), SCORE_ROWS)
             acc[where, :] += lax.dot_general(
                 xc[where, cols(c)], scaled[:, :width], NT, preferred_element_type=F32
             ) + lax.dot_general(xc[where, cols(c, half)], scaled[:, width:], NT, preferred_element_type=F32)
             return 0
 
-        lax.fori_loop(0, rows // 384, block, 0)
+        lax.fori_loop(0, rows // SCORE_ROWS, block, 0)
 
     def first(n, _):
         @pl.when(n < CHUNKS)
         def _():
             y_copy(n).wait_recv()
             ring_copy(0, n).start()
+            ring_copy(1, n).start()
             sib_copy(0, n).start()
 
-        for t in range(1, 4):
-            c = n - 2 * t
-
-            @pl.when((c >= 0) & (c < CHUNKS))
-            def _():
-                ring_copy(t - 1, c).wait_recv()
-                if t < 3:
-                    ring_copy(t, c).start()
-                sib_copy(t, c).start()
+        near = n - LAG
+
+        @pl.when((near >= 0) & (near < CHUNKS))
+        def _():
+            ring_copy(0, near).wait_recv()
+            ring_copy(2, near).start()
+            sib_copy(1, near).start()
+            ring_copy(1, near).wait_recv()
+            sib_copy(3, near).start()
+
+        far = n - 2 * LAG
+
+        @pl.when((far >= 0) & (far < CHUNKS))
+        def _():
+            ring_copy(2, far).wait_recv()
+            sib_copy(2, far).start()
 
         c = n // 2
         part_of = n % 2
-
-        @pl.when(part_of == 0)
-        def _():
+        shifting = n < 2 * CHUNKS
+
+        @pl.when(shifting & (part_of == 0))
+        def _():
+            @pl.when(c + 2 < CHUNKS)
+            def _():
+                start_images(c + 2, 0)
+
             img_copy(0, c).wait()
             img_copy(1, c).wait()
 
-        @pl.when(c == share)
+        @pl.when(shifting & (c == share))
         def _():
             shift_chunk(c, part_of, True)
 
-        @pl.when(c != share)
+        @pl.when(shifting & (c != share))
         def _():
             shift_chunk(c, part_of, False)
 
-        @pl.when(n >= CHUNKS)
-        def _():
-            score(n - CHUNKS)
+        ready = n - 2 * LAG - 2
+
+        @pl.when((ready >= 0) & (ready < CHUNKS))
+        def _():
+            score(ready)
 
         return 0
 
-    lax.fori_loop(0, 2 * CHUNKS, first, 0)
-
+    lax.fori_loop(0, max(2 * LAG + 2 + CHUNKS, 2 * CHUNKS), first, 0)
 
     penalty = csq[0:8, :]
     for r in range(rows // 128):
@@ -278,9 +295,9 @@
     for k in range(8):
         total = total + msgs[k, 1:2, :] * jnp.exp(msgs[k, 0:1, :] - top)
         offset = offset + msgs[k, 2:3, :]
-    loglik[...] = top + jnp.log(total) - offset
+    loglik[...] = (top + jnp.log(total) - offset).reshape(rows)
     wt[...] = (jnp.exp(scores[...] - top) / total).astype(BF16)
-    onehot = jnp.where(lax.broadcasted_iota(jnp.int32, (128, rows), 0) == bin_row[...], 1.0, 0.0).astype(BF16)
+    onehot = jnp.where(lax.broadcasted_iota(jnp.int32, (128, rows), 0) == bin_row[...].reshape(1, rows), 1.0, 0.0).astype(BF16)
     bins = lax.dot_general(wt[...], onehot, NT, preferred_element_type=F32)
     for u in range(16):
         binsend[u] = bins[u * 8 : u * 8 + 8, :]
@@ -306,9 +323,6 @@
 
     def everything(route):
         return pl.ds(route * middle, middle)
-
-    def target(t):
-        return (x + (1 + t) * turn) % 4
 
     def part_copy(route, d, q=None):
         q = at_step(route, d) if q is None else q
@@ -317,12 +331,16 @@
             psend.at[route], precv.at[route, d], {"particle": sibling},
         )
 
+    onward, across, behind = (x + 3 * turn) % 4, (x + 2) % 4, (x + turn) % 4
+    goal = (across, behind, onward)
+    to = (nxt, prv, nxt)
+
     def ring_a_copy(t, d, q=None):
         p = local(d) if q is None else q
         q = at_step(0, d) if q is None else q
         return remote(
-            part.at[core, target(t), :, :, q], ring_a.at[t, :, :, p],
-            qsend.at[t], arecv.at[t, d], {"particle": nxt},
+            part.at[core, goal[t], :, :, q], ring_a.at[t, :, :, p],
+            qsend.at[t], arecv.at[t, d], {"particle": to[t]},
         )
 
     def fin_copy(d, q=None):
@@ -343,16 +361,21 @@
         p = everything(0) if whole else local(d)
         q = everything(1) if whole else at_step(1, d)
         return remote(
-            part.at[core, target(t), yh, :, q], ring_b.at[t, :, p],
-            qsend.at[5 + t], brecv_ring.at[t, d], {"particle": nxt},
-        )
-
-    def gain(i, j, q, other):
-        part[core, i, j, :, q] = (part[core, i, j, :, q].astype(F32) + other.astype(F32)).astype(BF16)
-
-    def result(route, d, other):
+            part.at[core, goal[t], yh, :, q], ring_b.at[t, :, p],
+            qsend.at[5 + t], brecv_ring.at[t, d], {"particle": to[t]},
+        )
+
+    def gain(i, j, q, *others):
+        value = part[core, i, j, :, q].astype(F32)
+        for other in others:
+            value = value + other.astype(F32)
+        part[core, i, j, :, q] = value.astype(BF16)
+
+    def result(route, d, *others):
         q = at_step(route, d)
-        both = part[core, x, yh, :, q].astype(F32) + other.astype(F32)
+        both = part[core, x, yh, :, q].astype(F32)
+        for other in others:
+            both = both + other.astype(F32)
         for h in range(2):
             at = pl.ds(pl.multiple_of(h * half + route * middle + d * span_of, span_of), span_of)
             below = jnp.broadcast_to(tau[:, at], (8, span_of))
@@ -405,6 +428,7 @@
                 lax.fori_loop(0, 4, add, 0)
                 if route == 0:
                     ring_a_copy(0, d1).start()
+                    ring_a_copy(1, d1).start()
                 else:
                     cross_copy(d1).start()
 
@@ -414,36 +438,26 @@
         def _():
             ring_a_copy(0, d2).wait_recv()
             for j in range(2):
-                gain(target(1), j, at_step(0, d2), ring_a[0, j, :, local(d2)])
-            ring_a_copy(1, d2).start()
+                gain(onward, j, at_step(0, d2), ring_a[0, j, :, local(d2)])
+            ring_a_copy(2, d2).start()
             cross_copy(d2).wait_recv()
             for i in range(4):
                 gain(i, yh, at_step(1, d2), cross[i, :, local(d2)])
             ring_b_copy(0, d2).start()
+            ring_b_copy(1, d2).start()
 
         d3, on3 = stage(n, 5)
 
         @on3
         def _():
+            ring_b_copy(0, d3).wait_recv()
+            gain(onward, yh, at_step(1, d3), ring_b[0, :, local(d3)])
+            ring_b_copy(2, d3).start()
             ring_a_copy(1, d3).wait_recv()
+            ring_a_copy(2, d3).wait_recv()
             for j in range(2):
-                gain(target(2), j, at_step(0, d3), ring_a[1, j, :, local(d3)])
-            ring_a_copy(2, d3).start()
-            ring_b_copy(0, d3).wait_recv()
-            gain(target(1), yh, at_step(1, d3), ring_b[0, :, local(d3)])
-            ring_b_copy(1, d3).start()
-
-        d4, on4 = stage(n, 7)
-
-        @on4
-        def _():
-            ring_a_copy(2, d4).wait_recv()
-            for j in range(2):
-                gain(x, j, at_step(0, d4), ring_a[2, j, :, local(d4)])
-            fin_copy(d4).start()
-            ring_b_copy(1, d4).wait_recv()
-            gain(target(2), yh, at_step(1, d4), ring_b[1, :, local(d4)])
-            ring_b_copy(2, d4).start()
+                gain(x, j, at_step(0, d3), ring_a[1, j, :, local(d3)], ring_a[2, j, :, local(d3)])
+            fin_copy(d3).start()
 
         @pl.when(n == 5)
         def _():
@@ -453,18 +467,19 @@
                 whole = whole + binrecv[k]
             binsum[...] = whole
 
-        d5, on5 = stage(n, 9)
-
-        @on5
-        def _():
-            fin_copy(d5).wait_recv()
-            result(0, d5, fin[:, local(d5)])
-            ring_b_copy(2, d5).wait_recv()
-            result(1, d5, ring_b[2, :, local(d5)])
+        d4, on4 = stage(n, 7)
+
+        @on4
+        def _():
+            fin_copy(d4).wait_recv()
+            result(0, d4, fin[:, local(d4)])
+            ring_b_copy(1, d4).wait_recv()
+            ring_b_copy(2, d4).wait_recv()
+            result(1, d4, ring_b[1, :, local(d4)], ring_b[2, :, local(d4)])
 
         return 0
 
-    lax.fori_loop(0, steps + 9, second, 0)
+    lax.fori_loop(0, steps + 7, second, 0)
 
     full = pl.ds(0, half)
     y_copy(0, full).wait_send()
@@ -497,7 +512,7 @@
         kernel,
         out_shape=(
             jax.ShapeDtypeStruct(bank.shape, F32),
-            jax.ShapeDtypeStruct((1, rows), F32),
+            jax.ShapeDtypeStruct((rows,), F32),
         ),
         in_specs=[pl.BlockSpec(memory_space=pl.ANY)] + [whole] * 7,
         out_specs=(whole, whole),
@@ -552,9 +567,9 @@
         name="expectation",
     )(
         images, ctf_table, noise_var.reshape(1, size), tau.reshape(1, size), bank, wave,
-        shifts.T, defocus[None, :],
+        shifts.T, defocus,
     )
-    return recon, loglik.reshape(rows)
+    return recon, loglik
 
 
 def solution(mesh):

time: 99.1 us -> 91.1 us (0.919)
  Pallas kernels: 93.8 us -> 87.1 us
  other arithmetic: 1.29 us -> 0 us
    pallas_call x1, Pallas kernels: 93.8 us -> 87.1 us  [body(): pl.pallas_call(kernel, out_shape=(jax.ShapeDtypeStruct(bank.shape, F32),...]
    pallas_call x1 -> x0, other arithmetic: 1.29 us -> none  [body(): pl.pallas_call(kernel, out_shape=(jax.ShapeDtypeStruct(bank.shape, F32),...]
    broadcast_in_dim x1 -> x0, local copies, waits for them, and re-layouts: 1.27 us -> none  [body(): defocus[None, :]]
    unnamed x1 -> x2, local copies, waits for them, and re-layouts: 1.87 us -> 3.14 us
where the time goes in v3:
time: 91.1 us; the launch traced here: 90.9 us
  Pallas kernels  87.1 us (96%)
  local copies, waits for them, and re-layouts  3.14 us (3%)
    pallas_call x1, Pallas kernels, body(): pl.pallas_call(kernel, out_shape=(jax.ShapeDtypeStruct(bank.shape, F32),...  87.1 us
    unnamed x2, local copies, waits for them, and re-layouts  3.14 us

profile of v3, /device:TPU:0, one launch (start us, length us, event | category | flops | bytes accessed | tf_op | source)
XLA Modules:
  0.0 90.9 jit_solution(9772985296511547719)
XLA Ops:
  0.6 87.1 %expectation.1 = (f32[2,4,16384]{2,1,0:T(4,128)}, f32[768]{0:T(1024)}) custom-call(bf16[768,16384]{1,0:T(8,128)(2,1)} %images.1, f32[8,16384]{1,0:T(8,128)} %ctf.1, f32[1,16384]{1,0:T(1,128)} %bitcast.3, f32[1,16384]{1,0:T(1,128)} %bitcast.4, bf16[2,4,16384]{2,1,0:T(4,128)(2,1)} %bank.1, f32[1,128]{1,0:T(1,128)} %constant.2.clone.wave, s32[2,768]{1,0:T(2,128)} %bitcast.5, ...), custom_call_target="tpu_custom_call" | custom-call | tf_op jit(solution)/shard_map/expectation/pallas_call | solution.py:511
  87.7 1.9 %copy.12 = f32[2,4,16384]{2,1,0:T(4,128)} copy(f32[2,4,16384]{2,1,0:T(4,128)} %get-tuple-element.4) | data formatting | bytes 1048576
  89.6 1.3 %copy.13 = f32[768]{0:T(1024)} copy(f32[768]{0:T(1024)} %get-tuple-element.5) | data formatting | bytes 6144

commit v4 on v3

--- a/solution.py
+++ b/solution.py
@@ -12,8 +12,10 @@
 BF16 = jnp.bfloat16
 NT = (((1,), (1,)), ((), ()))
 CHUNKS = 8
-GROUP = 32
-LAG = 3
+GROUP = 64
+LAG = 4
+STEPS = 4
+STAGES = (1, 3, 5, 7)
 SCORE_ROWS = 768
 
 
@@ -269,15 +271,17 @@
     lax.fori_loop(0, max(2 * LAG + 2 + CHUNKS, 2 * CHUNKS), first, 0)
 
     penalty = csq[0:8, :]
-    for r in range(rows // 128):
+    lanes = rows // 128
+    msg[...] = jnp.zeros_like(msg)
+    for r in range(lanes):
         span = slice(r * 128, (r + 1) * 128)
         block_scores = acc[span, 0:128] + acc[span, 128:256] - pick_rows(penalty, bin_lanes[span, :])
-        scores[:, span] = block_scores.T
-        msg[2:3, span] = jnp.sum(off[span, :].T, axis=0, keepdims=True)
-    local_top = jnp.max(scores[...], axis=0, keepdims=True)
-    msg[0:1, :] = local_top
-    msg[1:2, :] = jnp.sum(jnp.exp(scores[...] - local_top), axis=0, keepdims=True)
-    msg[3:8, :] = jnp.zeros((5, rows), F32)
+        block_scores = block_scores.T
+        scores[:, span] = block_scores
+        block_top = jnp.max(block_scores, axis=0, keepdims=True)
+        msg[r : r + 1, :] = block_top
+        msg[8 + r : 9 + r, :] = jnp.sum(jnp.exp(block_scores - block_top), axis=0, keepdims=True)
+        msg[16 + r : 17 + r, :] = jnp.sum(off[span, :].T, axis=0, keepdims=True)
 
     def share_copy(k):
         return remote(msg, msgs.at[k], msend.at[k], mrecv.at[k], share_device((share + k) % 8))
@@ -287,16 +291,19 @@
     msgs[0] = msg[...]
     for k in range(1, 8):
         share_copy(k).wait_recv()
-    top = msgs[0, 0:1, :]
+    top = msgs[0, 0:8, :]
     for k in range(1, 8):
-        top = jnp.maximum(top, msgs[k, 0:1, :])
+        top = jnp.maximum(top, msgs[k, 0:8, :])
     total = jnp.zeros_like(top)
     offset = jnp.zeros_like(top)
     for k in range(8):
-        total = total + msgs[k, 1:2, :] * jnp.exp(msgs[k, 0:1, :] - top)
-        offset = offset + msgs[k, 2:3, :]
-    loglik[...] = (top + jnp.log(total) - offset).reshape(rows)
-    wt[...] = (jnp.exp(scores[...] - top) / total).astype(BF16)
+        total = total + msgs[k, 8:16, :] * jnp.exp(msgs[k, 0:8, :] - top)
+        offset = offset + msgs[k, 16:24, :]
+    found = top + jnp.log(total) - offset
+    for r in range(lanes):
+        span = slice(r * 128, (r + 1) * 128)
+        loglik[span] = found[r : r + 1, :].reshape(128)
+        wt[:, span] = (jnp.exp(scores[:, span] - top[r : r + 1, :]) / total[r : r + 1, :]).astype(BF16)
     onehot = jnp.where(lax.broadcasted_iota(jnp.int32, (128, rows), 0) == bin_row[...].reshape(1, rows), 1.0, 0.0).astype(BF16)
     bins = lax.dot_general(wt[...], onehot, NT, preferred_element_type=F32)
     for u in range(16):
@@ -310,10 +317,10 @@
     for k in range(1, 16):
         bin_copy(k).start()
 
-    steps = CHUNKS
+    steps = STEPS
     middle = half // 2
     span_of = middle // steps
-    sub = min(256, span_of)
+    sub = min(512, span_of)
 
     def at_step(route, d):
         return pl.ds(pl.multiple_of(route * middle + d * span_of, span_of), span_of)
@@ -412,7 +419,7 @@
             part_copy(0, n).start()
             part_copy(1, n).start()
 
-        d1, on1 = stage(n, 1)
+        d1, on1 = stage(n, STAGES[0])
 
         @on1
         def _():
@@ -432,7 +439,7 @@
                 else:
                     cross_copy(d1).start()
 
-        d2, on2 = stage(n, 3)
+        d2, on2 = stage(n, STAGES[1])
 
         @on2
         def _():
@@ -446,7 +453,7 @@
             ring_b_copy(0, d2).start()
             ring_b_copy(1, d2).start()
 
-        d3, on3 = stage(n, 5)
+        d3, on3 = stage(n, STAGES[2])
 
         @on3
         def _():
@@ -459,7 +466,7 @@
                 gain(x, j, at_step(0, d3), ring_a[1, j, :, local(d3)], ring_a[2, j, :, local(d3)])
             fin_copy(d3).start()
 
-        @pl.when(n == 5)
+        @pl.when(n == STAGES[3] - 1)
         def _():
             whole = binsend[own]
             for k in range(1, 16):
@@ -467,7 +474,7 @@
                 whole = whole + binrecv[k]
             binsum[...] = whole
 
-        d4, on4 = stage(n, 7)
+        d4, on4 = stage(n, STAGES[3])
 
         @on4
         def _():
@@ -479,7 +486,7 @@
 
         return 0
 
-    lax.fori_loop(0, steps + 7, second, 0)
+    lax.fori_loop(0, steps + STAGES[3], second, 0)
 
     full = pl.ds(0, half)
     y_copy(0, full).wait_send()
@@ -497,6 +504,11 @@
         share_copy(k).wait_send()
     for k in range(1, 16):
         bin_copy(k).wait_send()
+
+
+def hand_over(recon, loglik, recon_out, loglik_out):
+    recon_out[...] = recon[...]
+    loglik_out[...] = loglik[...]
 
 
 def body(images, ctf_table, defocus, shifts, noise_var, tau, bank):
@@ -531,8 +543,8 @@
             vmem((128, size // CHUNKS), BF16),
             vmem((128, rows), F32),
             vmem((128, rows), BF16),
-            vmem((8, rows), F32),
-            vmem((8, 8, rows), F32),
+            vmem((24, 128), F32),
+            vmem((8, 24, 128), F32),
             vmem((16, 8, 128), F32),
             vmem((16, 8, 128), F32),
             vmem((8, 128), F32),
@@ -554,12 +566,12 @@
             dma((16,)),
             dma((16,)),
             dma((2,)),
-            dma((2, CHUNKS)),
+            dma((2, STEPS)),
             dma((8,)),
-            dma((3, CHUNKS)),
-            dma((3, CHUNKS)),
-            dma((CHUNKS,)),
-            dma((CHUNKS,)),
+            dma((3, STEPS)),
+            dma((3, STEPS)),
+            dma((STEPS,)),
+            dma((STEPS,)),
         ],
         compiler_params=pltpu.CompilerParams(
             collective_id=0, has_side_effects=True, vmem_limit_bytes=60 * 1024 * 1024
@@ -569,6 +581,13 @@
         images, ctf_table, noise_var.reshape(1, size), tau.reshape(1, size), bank, wave,
         shifts.T, defocus,
     )
+    recon, loglik = pl.pallas_call(
+        hand_over,
+        out_shape=(jax.ShapeDtypeStruct(bank.shape, F32), jax.ShapeDtypeStruct((rows,), F32)),
+        in_specs=[whole, whole],
+        out_specs=(whole, whole),
+        name="hand_over",
+    )(recon, loglik)
     return recon, loglik
 
 

time: 91.1 us -> 84.7 us (0.930)
  Pallas kernels: 87.1 us -> 83.8 us
  local copies, waits for them, and re-layouts: 3.14 us -> 0 us
    pallas_call x1, Pallas kernels: 87.1 us -> 81.9 us  [body(): pl.pallas_call(kernel, out_shape=(jax.ShapeDtypeStruct(bank.shape, F32),...]
    unnamed x2 -> x0, local copies, waits for them, and re-layouts: 3.14 us -> none
    pallas_call x0 -> x1, Pallas kernels: none -> 1.87 us  [body(): pl.pallas_call(hand_over, out_shape=(jax.ShapeDtypeStruct(bank.shape, F32...]
where the time goes in v4:
time: 84.7 us; the launch traced here: 84.4 us
  Pallas kernels  83.8 us (99%)
    pallas_call x1, Pallas kernels, body(): pl.pallas_call(kernel, out_shape=(jax.ShapeDtypeStruct(bank.shape, F32),...  81.9 us
    pallas_call x1, Pallas kernels, body(): pl.pallas_call(hand_over, out_shape=(jax.ShapeDtypeStruct(bank.shape, F32...  1.87 us

profile of v4, /device:TPU:0, one launch (start us, length us, event | category | flops | bytes accessed | tf_op | source)
XLA Modules:
  0.0 84.4 jit_solution(17508360498531608971)
XLA Ops:
  0.6 81.9 %expectation.1 = (f32[2,4,16384]{2,1,0:T(4,128)}, f32[768]{0:T(1024)}) custom-call(bf16[768,16384]{1,0:T(8,128)(2,1)} %images.1, f32[8,16384]{1,0:T(8,128)} %ctf.1, f32[1,16384]{1,0:T(1,128)} %bitcast.3, f32[1,16384]{1,0:T(1,128)} %bitcast.4, bf16[2,4,16384]{2,1,0:T(4,128)(2,1)} %bank.1, f32[1,128]{1,0:T(1,128)} %constant.2.clone.wave, s32[2,768]{1,0:T(2,128)} %bitcast.5, ...), custom_call_target="tpu_custom_call" | custom-call | tf_op jit(solution)/shard_map/expectation/pallas_call | solution.py:523
  82.6 1.9 %hand_over.1 = (f32[2,4,16384]{2,1,0:T(4,128)}, f32[768]{0:T(1024)}) custom-call(f32[2,4,16384]{2,1,0:T(4,128)} %get-tuple-element.4.recon, f32[768]{0:T(1024)} %get-tuple-element.5.loglik), custom_call_target="tpu_custom_call" | custom-call | tf_op jit(solution)/shard_map/hand_over/pallas_call | solution.py:584
